TPU v7x, 128 devices: a whole 4x4x4 slice. The times are simulated.
128 devices in a mesh: seg: 8 (over x_hi, z), seq: 16 (over x_lo, y, core).
Axes of the slice: x: 4 (x_hi: 2, x_lo: 2; x = x_hi * 2 + x_lo), y: 4, z: 4, core: 2. Of those that a mesh axis runs over, the one named last changes fastest.
Arguments:
- keyframe_latents: bfloat16 [8, 2048, 1536], P('seg', 'seq'), may hold values from -24 to 24
- keyframe_steps: int32 [8], P('seg'), may hold values from 0 to 63
- infill_latents: bfloat16 [8, 2, 2048, 1536], P('seg', None, 'seq'), may hold values from -24 to 24
- infill_steps: int32 [8, 2], P('seg'), may hold values from 0 to 63
- bounds: int32 [8, 2], P('seg'), may hold values from 0 to 7, as said below
- shift_table: float32 [64, 1536], replicated, may hold values from -4 to 4
- scale_table: float32 [64, 1536], replicated, may hold values from -0.5 to 1.5
- gate_table: float32 [64, 1536], replicated, may hold values from 0.5 to 2.5
- query_weight: bfloat16 [1536, 2048], P(None, 'seq'), may hold values from -0.15625 to 0.15625
- key_weight: bfloat16 [1536, 2048], P(None, 'seq'), may hold values from -0.15625 to 0.15625
- value_weight: bfloat16 [1536, 2048], P(None, 'seq'), may hold values from -0.15625 to 0.15625
- out_weight: bfloat16 [2048, 1536], P('seq'), may hold values from -0.125 to 0.125
- query_gain: float32 [128], replicated, may hold values from 0.5 to 2
- key_gain: float32 [128], replicated, may hold values from 0.5 to 2
Outputs:
- keyframe_out: bfloat16 [8, 2048, 1536], P('seg', 'seq')
- infill_out: bfloat16 [8, 2, 2048, 1536], P('seg', None, 'seq')
Inputs may be any that keep to these rules, and one draw needn't show every extreme that they name: `bounds`: the two keyframes of a segment differ.
All inputs are finite; a program needn't handle non-finite values.
Results may differ from a plain program's by a relative error of at most 0.0052.
Values may be sent and summed in bfloat16 or wider, within the bound.
A program may use at most 192 MiB of HBM per device.

v0:
```python
import math
import jax
import jax.numpy as jnp
from jax import lax
from jax.sharding import PartitionSpec as P

HEAD = 128
EPSILON = 1e-06


def lookup(steps, table):
    entries = table.shape[0]
    onehot = (steps[:, None] == jnp.arange(entries, dtype=jnp.int32)[None, :]).astype(jnp.float32)
    return jnp.dot(onehot, table, precision=lax.Precision.HIGHEST)


def modulate(latents, steps, shift_table, scale_table):
    shifts = lookup(steps, shift_table)
    scales = lookup(steps, scale_table)
    values = latents.astype(jnp.float32)
    center = values - jnp.mean(values, axis=-1, keepdims=True)
    normed = center * lax.rsqrt(jnp.mean(center * center, axis=-1, keepdims=True) + EPSILON)
    return (normed * (1.0 + scales[:, None, :]) + shifts[:, None, :]).astype(jnp.bfloat16)


def head_norm(projected, gain):
    flat_rows = projected.shape[0]
    shaped = projected.reshape(flat_rows, -1, gain.shape[0])
    normed = shaped * lax.rsqrt(jnp.mean(shaped * shaped, axis=-1, keepdims=True) + EPSILON) * gain
    return normed.reshape(flat_rows, -1).astype(jnp.bfloat16)


def project(modded, query_weight, key_weight, value_weight, query_gain, key_gain):
    frames, tokens, features = modded.shape
    flat = modded.reshape(frames * tokens, features)
    query_rows = head_norm(
        jnp.dot(flat, query_weight, preferred_element_type=jnp.float32), query_gain
    )
    key_rows = head_norm(jnp.dot(flat, key_weight, preferred_element_type=jnp.float32), key_gain)
    value_rows = jnp.dot(flat, value_weight, preferred_element_type=jnp.float32).astype(
        jnp.bfloat16
    )
    stacked = jnp.stack([query_rows, key_rows, value_rows], axis=1)
    return stacked.reshape(frames, tokens, 3, -1)


def attend(query_rows, key_rows, value_rows):
    length, columns = query_rows.shape
    head_count = columns // HEAD
    block_rows = math.gcd(512, length)
    query_blocks = query_rows.reshape(length // block_rows, block_rows, head_count, HEAD)
    key_heads = key_rows.reshape(-1, head_count, HEAD)
    value_heads = value_rows.reshape(-1, head_count, HEAD)

    def one_block(queries):
        scores = jnp.einsum(
            "qhd,khd->hqk", queries, key_heads, preferred_element_type=jnp.float32
        ) * (1.0 / math.sqrt(HEAD))
        powers = jnp.exp(scores)
        weights = (powers / jnp.sum(powers, axis=-1, keepdims=True)).astype(jnp.bfloat16)
        return jnp.einsum(
            "hqk,khd->qhd", weights, value_heads, preferred_element_type=jnp.float32
        ).astype(jnp.bfloat16)

    return lax.map(one_block, query_blocks).reshape(length, columns)


def local(
    keyframe_latents,
    keyframe_steps,
    infill_latents,
    infill_steps,
    bounds,
    shift_table,
    scale_table,
    gate_table,
    query_weight,
    key_weight,
    value_weight,
    out_weight,
    query_gain,
    key_gain,
):
    out_full = lax.all_gather(out_weight, "seq", axis=0, tiled=True)

    def to_heads(modded):
        return project(
            lax.all_gather(modded, "seq", axis=1, tiled=True),
            query_weight,
            key_weight,
            value_weight,
            query_gain,
            key_gain,
        )

    def finish(latents, steps, heads_out):
        token_side = lax.all_to_all(heads_out, "seq", split_axis=1, concat_axis=2, tiled=True)
        frames, tokens, columns = token_side.shape
        branch = jnp.dot(
            token_side.reshape(frames * tokens, columns),
            out_full,
            preferred_element_type=jnp.float32,
        ).reshape(latents.shape)
        gates = lookup(steps, gate_table)
        return (latents.astype(jnp.float32) + gates[:, None, :] * branch).astype(jnp.bfloat16)

    key_heads = to_heads(modulate(keyframe_latents, keyframe_steps, shift_table, scale_table))
    key_att = lax.map(
        lambda frame_data: attend(frame_data[:, 0], frame_data[:, 1], frame_data[:, 2]), key_heads
    )
    keyframe_out = finish(keyframe_latents, keyframe_steps, key_att)
    cond_all = lax.all_gather(key_heads[:, :, 1:], "seg", axis=0, tiled=True)
    segment_count = bounds.shape[0]
    length = cond_all.shape[1]
    picked = jnp.take(cond_all, bounds.reshape(-1), axis=0)
    picked = picked.reshape(segment_count, 2 * length, 2, cond_all.shape[3])
    frames = infill_latents.shape[1]
    flat_latents = infill_latents.reshape(
        segment_count * frames, infill_latents.shape[2], infill_latents.shape[3]
    )
    flat_steps = infill_steps.reshape(-1)
    infill_heads = to_heads(modulate(flat_latents, flat_steps, shift_table, scale_table))
    bounding = jnp.repeat(picked, frames, axis=0)

    def infill_frame(bundle):
        own_frame, cond_frame = bundle
        key_rows = jnp.concatenate([own_frame[:, 1], cond_frame[:, 0]], axis=0)
        value_rows = jnp.concatenate([own_frame[:, 2], cond_frame[:, 1]], axis=0)
        return attend(own_frame[:, 0], key_rows, value_rows)

    infill_att = lax.map(infill_frame, (infill_heads, bounding))
    infill_out = finish(flat_latents, flat_steps, infill_att).reshape(infill_latents.shape)
    return (keyframe_out, infill_out)


def solution(mesh):
    return jax.shard_map(
        local,
        mesh=mesh,
        in_specs=(
            P("seg", "seq", None),
            P("seg"),
            P("seg", None, "seq", None),
            P("seg", None),
            P("seg", None),
            P(),
            P(),
            P(),
            P(None, "seq"),
            P(None, "seq"),
            P(None, "seq"),
            P("seq", None),
            P(),
            P(),
        ),
        out_specs=(P("seg", "seq", None), P("seg", None, "seq", None)),
        check_vma=False,
    )
```

profile of v0, /device:TPU:1, one launch (start us, length us, event | category | flops | bytes accessed | tf_op | source)
XLA Modules:
  0.0 350.8 jit_solution(5878969197463367039)
XLA Ops:
  8.0 1.3 convolution_reduce_fusion.1
  9.3 1.2 convert_reduce_fusion.1
  10.5 1.2 fusion.68
  11.7 1.3 convolution_reduce_fusion
  13.0 2.1 fusion.71
  16.2 1.3 fusion.65
  17.6 43.5 %all-gather.5.cloned.1.call-done = bf16[1,2048,1536]{2,1,0:T(8,128)(2,1)} async-done(((bf16[1,128,1536]{2,1,0:T(8,128)(2,1)}), bf16[1,2048,1536]{2,1,0:T(8,128)(2,1)}) %all-gather.5.cloned.1.call-update) | async-done | bytes 6291472 | tf_op jit(solution)/shard_map/all_gather | solution.py:88
  61.1 5.0 %multiply_reduce_fusion.2 = (f32[2048]{0:T(1024)S(1)}, f32[2048,128]{0,1:T(8,128)S(1)}) fusion(bf16[1536,128]{1,0:T(8,128)(2,1)S(1)} %copy-done.11, bf16[1,2048,1536]{2,1,0:T(8,128)(2,1)} %all-gather.5.cloned.1.call-done), kind=kOutput, calls=%fused_computation.81 | convolution fusion | flops 805828608 | bytes 7741440 | tf_op jit(solution)/shard_map/dot_general | solution.py:39
  66.5 4.8 %multiply_reduce_fusion.3 = (f32[2048]{0:T(1024)S(1)}, f32[2048,128]{1,0:T(8,128)S(1)}) fusion(bf16[1536,128]{1,0:T(8,128)(2,1)S(1)} %copy-done, bf16[1,2048,1536]{2,1,0:T(8,128)(2,1)} %all-gather.5.cloned.1.call-done), kind=kOutput, calls=%fused_computation.83 | convolution fusion | flops 805828608 | bytes 7741440 | tf_op jit(solution)/shard_map/dot_general | solution.py:37
  71.3 1.8 fusion.56
  74.1 1.1 slice.32
  75.9 1.0 multiply_convert_fusion.3
  76.9 7.0 %while.37 = (s32[]{:T(128)}, bf16[4,512,1,128]{3,1,2,0:T(8,128)(2,1)S(1)}, bf16[4,512,1,128]{3,1,2,0:T(8,128)(2,1)S(1)}, bf16[2048,1,128]{2,0,1:T(8,128)(2,1)S(1)}, bf16[2048,1,128]{2,0,1:T(8,128)(2,1)S(1)}, /*index=5*/s32[]{:T(128)}) while((s32[]{:T(128)}, bf16[4,512,1,128]{3,1,2,0:T(8,128)(2,1)S(1)}, bf16[4,512,1,128]{3,1,2,0:T(8,128)(2,1)S(1)}, ...), condition=%wide.region_6.0_spmd, body=%wide.region_4.6_spmd.sunk | while | flops 542178816 | bytes 9703501 | solution.py:65
  76.9 0.8 fusion.111
  77.8 0.9 fusion.112
  79.5 0.9 fusion.112
  81.3 0.9 fusion.112
  83.0 0.9 fusion.112
  84.0 8.1 %copy.65 = bf16[1,2048,128]{2,0,1:T(2,128)(2,1)S(1)} copy(bf16[1,2048,128]{2,1,0:T(8,128)(2,1)S(1)} %bitcast.242) | data formatting | bytes 1048576 | tf_op jit(solution)/shard_map/while/body/jit(dynamic_update_index_in_dim)/broadcast_in_dim | solution.py:108
  92.6 11.5 %reduce.21 = bf16[2048,128]{1,0:T(8,128)(2,1)S(1)} reduce(bf16[2048,1,128]{2,1,0:T(2,128)(2,1)S(1)} %bitcast.234, bf16[]{:T(256)} %broadcast.240), dimensions={1}, to_apply=%bitcast.196.reduce_sub_computation | reduce | bytes 1048578
  104.2 0.9 reshape.341
  105.1 5.4 %all-to-all-start = ((bf16[16,2,8192]{2,1,0:T(2,128)(2,1)}), bf16[16,2,8192]{2,1,0:T(2,128)(2,1)}, u32[]{:S(2)}, u32[]{:S(2)}) async-start(bf16[16,2,8192]{2,1,0:T(2,128)(2,1)} %reshape.341), calls=%async_computation | async-start | bytes 1048576 | tf_op jit(solution)/shard_map/all_to_all | solution.py:97
  110.5 31.3 %all-gather.9.cloned.1.call-done = bf16[2,2048,1536]{2,1,0:T(8,128)(2,1)} async-done(((bf16[2,128,1536]{2,1,0:T(8,128)(2,1)}), bf16[2,2048,1536]{2,1,0:T(8,128)(2,1)}) %all-gather.9.cloned.1.call-update) | async-done | bytes 12582928 | tf_op jit(solution)/shard_map/all_gather | solution.py:88
  141.8 6.7 %multiply_reduce_fusion.1 = (f32[4096]{0:T(1024)S(1)}, f32[4096,128]{1,0:T(8,128)S(1)}) fusion(bf16[4096,1536]{1,0:T(8,128)(2,1)} %bitcast.246, bf16[1536,128]{1,0:T(8,128)(2,1)S(1)} %copy-done), kind=kOutput, calls=%fused_computation.63 | convolution fusion | flops 1611657216 | bytes 15089664 | tf_op jit(solution)/shard_map/dot_general | solution.py:37
  148.5 1.6 copy-done.19
  150.1 3.5 %multiply_reduce_fusion = (f32[4096]{0:T(1024)S(1)}, f32[4096,128]{1,0:T(8,128)S(1)}) fusion(bf16[4096,1536]{1,0:T(8,128)(2,1)S(1)} %bitcast.247, bf16[1536,128]{1,0:T(8,128)(2,1)S(1)} %copy-done.12), kind=kOutput, calls=%fused_computation.61 | convolution fusion | flops 1611657216 | bytes 15089664 | tf_op jit(solution)/shard_map/dot_general | solution.py:39
  153.7 3.4 convolution_convert_fusion
  158.6 2.0 pad_maximum_fusion
  160.6 91.0 %all-gather.11.cloned.1.call-done = bf16[8,2048,2,128]{3,1,2,0:T(8,128)(2,1)} async-done(((bf16[1,2048,2,128]{3,1,2,0:T(8,128)(2,1)}), bf16[8,2048,2,128]{3,1,2,0:T(8,128)(2,1)}) %all-gather.11.cloned.1.call-update) | async-done | bytes 8388624 | tf_op jit(solution)/shard_map/all_gather | solution.py:112
  251.6 4.3 %gather_fusion = bf16[2,2048,2,128]{3,1,2,0:T(8,128)(2,1)S(1)} fusion(bf16[8,2048,2,128]{3,1,2,0:T(8,128)(2,1)} %all-gather.11.cloned.1.call-done, s32[1024]{0:T(1024)S(1)} %pad_clamp_fusion), kind=kCustom, calls=%fused_computation | custom fusion | bytes 4194312 | tf_op jit(solution)/shard_map/jit(_take)/gather | solution.py:115
  256.1 2.2 bitcast_select_fusion
  258.2 2.5 reshape.321
  260.7 51.7 %while.39 = (s32[]{:T(128)}, bf16[2,2048,128]{2,1,0:T(8,128)(2,1)}, bf16[2,2048,3,128]{3,1,2,0:T(8,128)(2,1)}, bf16[2,4096,2,128]{3,1,2,0:T(8,128)(2,1)}, s32[]{:T(128)}, /*index=5*/s32[]{:T(128)}, s32[]{:T(128)}) while((s32[]{:T(128)}, bf16[2,2048,128]{2,1,0:T(8,128)(2,1)}, bf16[2,2048,3,128]{3,1,2,0:T(8,128)(2,1)}, ...), condition=%wide.region_15.16_spmd, body=%wide.region_11.15_spmd.sunk | while | flops 1632697856 | bytes 73667344 | solution.py:131
  260.9 1.7 dynamic-slice_bitcast_fusion.4
  262.7 0.9 copy-done.2
  263.9 1.5 maximum_bitcast_fusion.4
  265.3 20.4 %while.40 = (s32[]{:T(128)}, bf16[4,512,1,128]{3,1,2,0:T(8,128)(2,1)S(1)}, bf16[4,512,1,128]{3,1,2,0:T(8,128)(2,1)S(1)}, bf16[6144,1,128]{2,0,1:T(8,128)(2,1)S(1)}, bf16[6144,1,128]{2,0,1:T(8,128)(2,1)}, /*index=5*/s32[]{:T(128)}) while((s32[]{:T(128)}, bf16[4,512,1,128]{3,1,2,0:T(8,128)(2,1)S(1)}, bf16[4,512,1,128]{3,1,2,0:T(8,128)(2,1)S(1)}, ...), condition=%wide.region_14.14_spmd, body=%wide.region_12.13_spmd.sunk | while | flops 1626406400 | bytes 34869352 | solution.py:65
  265.3 2.0 fusion.114
  267.4 3.1 fusion.115
  270.4 2.0 fusion.114
  272.5 3.1 fusion.115
  275.6 2.0 fusion.114
  277.6 3.1 fusion.115
  280.7 2.0 fusion.114
  282.7 3.1 fusion.115
  285.8 0.9 constant_dynamic-update-slice_fusion.2
  286.6 1.7 dynamic-slice_bitcast_fusion.4
  288.5 1.0 copy-done.2
  289.7 1.5 maximum_bitcast_fusion.4
  291.2 20.4 %while.40 = (s32[]{:T(128)}, bf16[4,512,1,128]{3,1,2,0:T(8,128)(2,1)S(1)}, bf16[4,512,1,128]{3,1,2,0:T(8,128)(2,1)S(1)}, bf16[6144,1,128]{2,0,1:T(8,128)(2,1)S(1)}, bf16[6144,1,128]{2,0,1:T(8,128)(2,1)}, /*index=5*/s32[]{:T(128)}) while((s32[]{:T(128)}, bf16[4,512,1,128]{3,1,2,0:T(8,128)(2,1)S(1)}, bf16[4,512,1,128]{3,1,2,0:T(8,128)(2,1)S(1)}, ...), condition=%wide.region_14.14_spmd, body=%wide.region_12.13_spmd.sunk | while | flops 1626406400 | bytes 34869352 | solution.py:65
  291.2 2.0 fusion.114
  293.2 3.1 fusion.115
  296.3 2.0 fusion.114
  298.3 3.1 fusion.115
  301.4 2.0 fusion.114
  303.4 3.1 fusion.115
  306.5 2.0 fusion.114
  308.6 3.1 fusion.115
  312.5 3.6 %copy.59 = bf16[2,2048,128]{2,0,1:T(2,128)(2,1)} copy(bf16[2,2048,128]{2,1,0:T(8,128)(2,1)} %get-tuple-element.88) | data formatting | bytes 2097152 | tf_op jit(solution)/shard_map/while | solution.py:131
  316.1 5.4 %all-to-all-start.1 = ((bf16[2,2048,128]{2,0,1:T(2,128)(2,1)}), bf16[2,2048,128]{2,0,1:T(2,128)(2,1)S(1)}, u32[]{:S(2)}, u32[]{:S(2)}) async-start(bf16[2,2048,128]{2,0,1:T(2,128)(2,1)} %copy.59), calls=%async_computation.1 | async-start | bytes 2097152 | tf_op jit(solution)/shard_map/all_to_all | solution.py:97
  322.1 2.3 reshape.342
  324.7 4.6 %fusion.52 = bf16[1,128,1536]{2,1,0:T(8,128)(2,1)} fusion(bf16[128,2048]{0,1:T(8,128)(2,1)S(1)} %bitcast.239, bf16[2048,1536]{1,0:T(8,128)(2,1)} %all-gather.7.cloned.1.call-done, bf16[1,128,1536]{2,1,0:T(8,128)(2,1)S(1)} %copy-done.7, f32[1536]{0:T(1024)S(1)} %convolution_reduce_fusion.2), kind=kOutput, calls=%fused_computation.55 | convolution fusion | flops 806092800 | bytes 7608320 | tf_op jit(solution)/shard_map/dot_general | solution.py:99
  329.3 8.1 %all-to-all-done.1 = bf16[2,2048,128]{2,0,1:T(2,128)(2,1)S(1)} async-done(((bf16[2,2048,128]{2,0,1:T(2,128)(2,1)}), bf16[2,2048,128]{2,0,1:T(2,128)(2,1)S(1)}, u32[]{:S(2)}, u32[]{:S(2)}) %all-to-all-start.1) | async-done | bytes 1048608 | tf_op jit(solution)/shard_map/all_to_all | solution.py:97
  338.6 5.5 %fusion.48 = bf16[1,2,128,1536]{3,2,1,0:T(8,128)(2,1)} fusion(bf16[2,128,2048]{2,1,0:T(8,128)(2,1)S(1)} %dot_general.69, bf16[2048,1536]{1,0:T(8,128)(2,1)} %all-gather.7.cloned.1.call-done, bf16[1,2,128,1536]{3,2,1,0:T(8,128)(2,1)S(1)} %copy-done.6, f32[2,1536]{1,0:T(2,128)S(1)} %fusion.77), kind=kOutput, calls=%fused_computation.53 | convolution fusion | flops 1612185600 | bytes 8925184 | tf_op jit(solution)/shard_map/dot_general | solution.py:99
  (115 shorter events, 11.5 us)
Async XLA Ops:
  7.2 59.3 %copy-start = (bf16[1536,128]{1,0:T(8,128)(2,1)S(1)}, bf16[1536,128]{1,0:T(8,128)(2,1)}, u32[]{:S(2)}) copy-start(bf16[1536,128]{1,0:T(8,128)(2,1)} %param.28) | copy-start | bytes 1179652
  7.2 8.0 %copy-start.5 = (bf16[1,2,128,1536]{3,2,1,0:T(8,128)(2,1)S(1)}, bf16[1,2,128,1536]{3,2,1,0:T(8,128)(2,1)}, u32[]{:S(2)}) copy-start(bf16[1,2,128,1536]{3,2,1,0:T(8,128)(2,1)} %param.22) | copy-start | bytes 2359300
  7.2 53.9 %all-gather.5.cloned.1.call-start = ((), (), s32[]{:S(2)}) async-start(), calls=%async_computation.2 | async-start | bytes 6684672 | tf_op jit(solution)/shard_map/all_gather | solution.py:88
  9.2 6.5 %copy-start.8 = (f32[64,1536]{1,0:T(8,128)S(1)}, f32[64,1536]{1,0:T(8,128)}, u32[]{:S(2)}) copy-start(f32[64,1536]{1,0:T(8,128)} %param.26) | copy-start | bytes 1179652
  9.2 6.5 %copy-start.13 = (s32[1,2]{1,0:T(1,128)S(1)}, s32[1,2]{1,0:T(1,128)}, u32[]{:S(2)}) copy-start(s32[1,2]{1,0:T(1,128)} %param.23) | copy-start | bytes 28
  9.3 6.7 %copy-start.9 = (f32[64,1536]{1,0:T(8,128)S(1)}, f32[64,1536]{1,0:T(8,128)}, u32[]{:S(2)}) copy-start(f32[64,1536]{1,0:T(8,128)} %param.25) | copy-start | bytes 1179652
  15.1 126.7 %all-gather.9.cloned.1.call-start = ((), (), s32[]{:S(2)}) async-start(), calls=%async_computation.4 | async-start | bytes 13369344 | tf_op jit(solution)/shard_map/all_gather | solution.py:88
  15.3 45.8 %copy-start.11 = (bf16[1536,128]{1,0:T(8,128)(2,1)S(1)}, bf16[1536,128]{1,0:T(8,128)(2,1)}, u32[]{:S(2)}) copy-start(bf16[1536,128]{1,0:T(8,128)(2,1)} %param.29) | copy-start | bytes 1179652
  17.5 234.1 %all-gather.11.cloned.1.call-start = ((), (), s32[]{:S(2)}) async-start(), calls=%async_computation.5 | async-start | bytes 9437184 | tf_op jit(solution)/shard_map/all_gather | solution.py:112
  66.4 4.9 %copy-start.4 = (bf16[1,2048,1536]{2,1,0:T(8,128)(2,1)S(1)}, bf16[1,2048,1536]{2,1,0:T(8,128)(2,1)}, u32[]{:S(2)}) copy-start(bf16[1,2048,1536]{2,1,0:T(8,128)(2,1)} %all-gather.5.cloned.1.call-done) | copy-start | bytes 18874372
  66.5 4.9 %copy-start.20 = (bf16[1536,128]{1,0:T(8,128)(2,1)S(1)}, bf16[1536,128]{1,0:T(8,128)(2,1)}, u32[]{:S(2)}) copy-start(bf16[1536,128]{1,0:T(8,128)(2,1)} %param.30) | copy-start | bytes 1179652
  71.3 1.8 copy-start.15
  71.3 2.2 copy-start.17
  74.0 1.7 copy-start.22
  75.2 249.6 %all-gather.7.cloned.1.call-start = ((), (), s32[]{:S(2)}) async-start(), calls=%async_computation.3 | async-start | bytes 6684672 | tf_op jit(solution)/shard_map/all_gather | solution.py:84
  105.1 211.0 %all-to-all-start = ((bf16[16,2,8192]{2,1,0:T(2,128)(2,1)}), bf16[16,2,8192]{2,1,0:T(2,128)(2,1)}, u32[]{:S(2)}, u32[]{:S(2)}) async-start(bf16[16,2,8192]{2,1,0:T(2,128)(2,1)} %reshape.341), calls=%async_computation | async-start | bytes 1048576 | tf_op jit(solution)/shard_map/all_to_all | solution.py:97
  141.8 6.7 %copy-start.12 = (bf16[1536,128]{1,0:T(8,128)(2,1)S(1)}, bf16[1536,128]{1,0:T(8,128)(2,1)}, u32[]{:S(2)}) copy-start(bf16[1536,128]{1,0:T(8,128)(2,1)} %param.29) | copy-start | bytes 1179652
  141.8 8.3 %copy-start.19 = (bf16[2,2048,1536]{2,1,0:T(8,128)(2,1)S(1)}, bf16[2,2048,1536]{2,1,0:T(8,128)(2,1)}, u32[]{:S(2)}) copy-start(bf16[2,2048,1536]{2,1,0:T(8,128)(2,1)} %all-gather.9.cloned.1.call-done) | copy-start | bytes 37748740
  150.1 3.5 %copy-start.21 = (bf16[1536,128]{1,0:T(8,128)(2,1)S(1)}, bf16[1536,128]{1,0:T(8,128)(2,1)}, u32[]{:S(2)}) copy-start(bf16[1536,128]{1,0:T(8,128)(2,1)} %param.30) | copy-start | bytes 1179652
  153.6 3.5 copy-start.16
  157.1 0.8 copy-start.18
  260.9 2.7 copy-start.2
  265.3 2.0 copy-start.3
  270.4 2.0 copy-start.3
  275.6 2.0 copy-start.3
  280.7 2.0 copy-start.3
  286.6 2.8 copy-start.2
  291.2 2.0 copy-start.3
  296.3 2.0 copy-start.3
  301.4 2.0 copy-start.3
  306.5 2.0 copy-start.3
  312.5 9.1 %copy-start.10 = (f32[64,1536]{1,0:T(8,128)S(1)}, f32[64,1536]{1,0:T(8,128)}, u32[]{:S(2)}) copy-start(f32[64,1536]{1,0:T(8,128)} %param.27) | copy-start | bytes 1179652
  312.5 9.3 %copy-start.14 = (s32[1,2]{1,0:T(1,128)S(1)}, s32[1,2]{1,0:T(1,128)}, u32[]{:S(2)}) copy-start(s32[1,2]{1,0:T(1,128)} %param.23) | copy-start | bytes 28
  316.1 21.2 %all-to-all-start.1 = ((bf16[2,2048,128]{2,0,1:T(2,128)(2,1)}), bf16[2,2048,128]{2,0,1:T(2,128)(2,1)S(1)}, u32[]{:S(2)}, u32[]{:S(2)}) async-start(bf16[2,2048,128]{2,0,1:T(2,128)(2,1)} %copy.59), calls=%async_computation.1 | async-start | bytes 2097152 | tf_op jit(solution)/shard_map/all_to_all | solution.py:97
  322.1 2.7 copy-start.7
  337.3 1.2 copy-start.6
  338.5 5.5 %copy-start.1 = (bf16[1536,128]{1,0:T(8,128)(2,1)S(1)}, bf16[1536,128]{1,0:T(8,128)(2,1)}, u32[]{:S(2)}) copy-start(bf16[1536,128]{1,0:T(8,128)(2,1)} %param.28) | copy-start | bytes 1179652
Sparse Core Ops, SparseCore 0:
  15.2 45.8 all-gather.4
  63.3 78.4 all-gather.8
  144.2 107.3 all-gather.10
  253.1 40.8 all-gather.6
where the time goes:
time: 357 us; the launch traced here: 351 us
  waiting for transfers between devices  174 us (49%)
  matrix products  86.5 us (24%)
  local copies, waits for them, and re-layouts  34.9 us (10%)
  other arithmetic  28.3 us (8%)
  between operations  15.3 us (4%)
  starting transfers between devices  11.5 us (3%)
    all_gather x1, waiting for transfers between devices, local(): cond_all = lax.all_gather(key_heads[:, :, 1:], 'seg', axis=0, tiled=True)  91 us
    all_gather x2, waiting for transfers between devices, to_heads(): lax.all_gather(modded, 'seq', axis=1, tiled=True)  74.8 us
    dot_general x12, matrix products, one_block(): jnp.einsum('hqk,khd->qhd', weights, value_heads, preferred_element_type=j...  28 us
    dot_general x12, matrix products, one_block(): jnp.einsum('qhd,khd->hqk', queries, key_heads, preferred_element_type=jnp...  19.6 us
    unnamed x1, other arithmetic  11.5 us
    dot_general x2, matrix products, project(): jnp.dot(flat, query_weight, preferred_element_type=jnp.float32)  11.5 us
    all_to_all x2, starting transfers between devices, finish(): lax.all_to_all(heads_out, 'seq', split_axis=1, concat_axis=2, tiled=True)  10.8 us
    dot_general x2, matrix products, finish(): jnp.dot(token_side.reshape(frames * tokens, columns), out_full, preferred...  10.1 us
  transfers between devices with their start and end apart: 6, of which 4 were waited for; matrix products, arithmetic and copies ran while one was open for 38% of the time, Pallas kernels for 0%

commit v1 on v0

--- a/solution.py
+++ b/solution.py
@@ -109,7 +109,12 @@
         lambda frame_data: attend(frame_data[:, 0], frame_data[:, 1], frame_data[:, 2]), key_heads
     )
     keyframe_out = finish(keyframe_latents, keyframe_steps, key_att)
-    cond_all = lax.all_gather(key_heads[:, :, 1:], "seg", axis=0, tiled=True)
+
+    def rest_the_chunk(local_values, ax_name):
+        local_next = jnp.stack([local_values for _ in range(lax.axis_size(ax_name))], axis=0)
+        return jnp.concatenate(lax.all_to_all(local_next, ax_name, 0, 0), 0)
+
+    cond_all = rest_the_chunk(key_heads[:, :, 1:], "seg")
     segment_count = bounds.shape[0]
     length = cond_all.shape[1]
     picked = jnp.take(cond_all, bounds.reshape(-1), axis=0)

time: 357 us -> 384 us (1.076)
  waiting for transfers between devices: 174 us -> 189 us
  starting transfers between devices: 11.5 us -> 18.7 us
    all_to_all x0 -> x1, waiting for transfers between devices: none -> 137 us  [rest_the_chunk(): return jnp.concatenate(lax.all_to_all(local_next, ax_name, 0, 0), 0)]
    all_gather x1 -> x0, waiting for transfers between devices: 91 us -> none  [local(): cond_all = lax.all_gather(key_heads[:, :, 1:], 'seg', axis=0, tiled=True)]
    all_gather x2, waiting for transfers between devices: 74.8 us -> 43.6 us  [to_heads(): lax.all_gather(modded, 'seq', axis=1, tiled=True)]
    all_to_all x0 -> x1, starting transfers between devices: none -> 6.69 us  [rest_the_chunk(): return jnp.concatenate(lax.all_to_all(local_next, ax_name, 0, 0), 0)]
    another operation x0 -> x1, local copies, waits for them, and re-layouts: none -> 4.87 us  [rest_the_chunk(): jnp.stack([local_values for _ in range(lax.axis_size(ax_name))], axis=0)]
  transfers between devices with their start and end apart: 6 -> 6, of which waited for: 4 -> 3; matrix products, arithmetic and copies ran while one was open for 38% -> 36% of each run, Pallas kernels for 0% -> 0%
where the time goes in v1:
time: 384 us; the launch traced here: 377 us
  waiting for transfers between devices  189 us (49%)
  matrix products  86.5 us (23%)
  local copies, waits for them, and re-layouts  38.6 us (10%)
  other arithmetic  28.2 us (7%)
  starting transfers between devices  18.7 us (5%)
  between operations  15.3 us (4%)
    all_to_all x1, waiting for transfers between devices, rest_the_chunk(): return jnp.concatenate(lax.all_to_all(local_next, ax_name, 0, 0), 0)  137 us
    all_gather x2, waiting for transfers between devices, to_heads(): lax.all_gather(modded, 'seq', axis=1, tiled=True)  43.6 us
    dot_general x12, matrix products, one_block(): jnp.einsum('hqk,khd->qhd', weights, value_heads, preferred_element_type=j...  28.1 us
    dot_general x12, matrix products, one_block(): jnp.einsum('qhd,khd->hqk', queries, key_heads, preferred_element_type=jnp...  19.6 us
    unnamed x1, other arithmetic  11.5 us
    dot_general x2, matrix products, project(): jnp.dot(flat, query_weight, preferred_element_type=jnp.float32)  11.5 us
    all_to_all x2, starting transfers between devices, finish(): lax.all_to_all(heads_out, 'seq', split_axis=1, concat_axis=2, tiled=True)  11.5 us
    dot_general x2, matrix products, finish(): jnp.dot(token_side.reshape(frames * tokens, columns), out_full, preferred...  10.1 us
  transfers between devices with their start and end apart: 6, of which 3 were waited for; matrix products, arithmetic and copies ran while one was open for 36% of the time, Pallas kernels for 0%

profile of v1, /device:TPU:1, one launch (start us, length us, event | category | flops | bytes accessed | tf_op | source)
XLA Modules:
  0.0 377.2 jit_solution(7273438107911995754)
XLA Ops:
  8.0 1.3 convolution_reduce_fusion.1
  9.3 1.2 convert_reduce_fusion.1
  10.5 1.2 fusion.68
  11.7 1.3 convolution_reduce_fusion
  13.0 2.1 fusion.71
  16.2 1.3 fusion.65
  17.5 43.6 %all-gather.4.cloned.1.call-done = bf16[1,2048,1536]{2,1,0:T(8,128)(2,1)} async-done(((bf16[1,128,1536]{2,1,0:T(8,128)(2,1)}), bf16[1,2048,1536]{2,1,0:T(8,128)(2,1)}) %all-gather.4.cloned.1.call-update) | async-done | bytes 6291472 | tf_op jit(solution)/shard_map/all_gather | solution.py:88
  61.1 5.0 %multiply_reduce_fusion.2 = (f32[2048]{0:T(1024)S(1)}, f32[2048,128]{0,1:T(8,128)S(1)}) fusion(bf16[1536,128]{1,0:T(8,128)(2,1)S(1)} %copy-done.11, bf16[1,2048,1536]{2,1,0:T(8,128)(2,1)} %all-gather.4.cloned.1.call-done), kind=kOutput, calls=%fused_computation.82 | convolution fusion | flops 805828608 | bytes 7741440 | tf_op jit(solution)/shard_map/dot_general | solution.py:39
  66.5 4.8 %multiply_reduce_fusion.3 = (f32[2048]{0:T(1024)S(1)}, f32[2048,128]{1,0:T(8,128)S(1)}) fusion(bf16[1536,128]{1,0:T(8,128)(2,1)S(1)} %copy-done, bf16[1,2048,1536]{2,1,0:T(8,128)(2,1)} %all-gather.4.cloned.1.call-done), kind=kOutput, calls=%fused_computation.84 | convolution fusion | flops 805828608 | bytes 7741440 | tf_op jit(solution)/shard_map/dot_general | solution.py:37
  71.3 1.8 fusion.56
  74.1 4.9 %stack.14 = bf16[8,1,2048,2,128]{4,2,3,1,0:T(8,128)(2,1)} broadcast(bf16[2048,2,128]{2,0,1:T(8,128)(2,1)S(1)} %slice_bitcast_fusion.4), dimensions={2,3,4} | broadcast | bytes 9437184 | tf_op jit(solution)/shard_map/stack | solution.py:114
  79.0 6.7 %all-to-all-start.1 = ((bf16[8,1,2048,2,128]{4,2,3,1,0:T(8,128)(2,1)}), bf16[8,1,2048,2,128]{4,2,3,1,0:T(8,128)(2,1)}, u32[]{:S(2)}, u32[]{:S(2)}) async-start(bf16[8,1,2048,2,128]{4,2,3,1,0:T(8,128)(2,1)} %stack.14), calls=%async_computation.1 | async-start | bytes 16777216 | tf_op jit(solution)/shard_map/all_to_all | solution.py:115
  86.6 1.0 multiply_convert_fusion.3
  87.6 7.0 %while.37 = (s32[]{:T(128)}, bf16[4,512,1,128]{3,1,2,0:T(8,128)(2,1)S(1)}, bf16[4,512,1,128]{3,1,2,0:T(8,128)(2,1)S(1)}, bf16[2048,1,128]{2,0,1:T(8,128)(2,1)S(1)}, bf16[2048,1,128]{2,0,1:T(8,128)(2,1)S(1)}, /*index=5*/s32[]{:T(128)}) while((s32[]{:T(128)}, bf16[4,512,1,128]{3,1,2,0:T(8,128)(2,1)S(1)}, bf16[4,512,1,128]{3,1,2,0:T(8,128)(2,1)S(1)}, ...), condition=%wide.region_6.0_spmd, body=%wide.region_4.6_spmd.sunk | while | flops 542178816 | bytes 9703501 | solution.py:65
  88.4 0.9 fusion.112
  89.4 0.8 fusion.111
  90.2 0.9 fusion.112
  92.0 0.9 fusion.112
  93.7 0.9 fusion.112
  94.6 8.1 %copy.66 = bf16[1,2048,128]{2,0,1:T(2,128)(2,1)S(1)} copy(bf16[1,2048,128]{2,1,0:T(8,128)(2,1)S(1)} %bitcast.245) | data formatting | bytes 1048576 | tf_op jit(solution)/shard_map/while/body/jit(dynamic_update_index_in_dim)/broadcast_in_dim | solution.py:108
  103.3 11.5 %reduce.21 = bf16[2048,128]{1,0:T(8,128)(2,1)S(1)} reduce(bf16[2048,1,128]{2,1,0:T(2,128)(2,1)S(1)} %bitcast.237, bf16[]{:T(256)} %broadcast.243), dimensions={1}, to_apply=%bitcast.199.reduce_sub_computation | reduce | bytes 1048578
  114.8 0.9 reshape.348
  115.8 137.4 %all-to-all-done.1 = bf16[8,1,2048,2,128]{4,2,3,1,0:T(8,128)(2,1)} async-done(((bf16[8,1,2048,2,128]{4,2,3,1,0:T(8,128)(2,1)}), bf16[8,1,2048,2,128]{4,2,3,1,0:T(8,128)(2,1)}, u32[]{:S(2)}, u32[]{:S(2)}) %all-to-all-start.1) | async-done | bytes 8388640 | tf_op jit(solution)/shard_map/all_to_all | solution.py:115
  253.1 5.7 %all-to-all-start = ((bf16[16,2,8192]{2,1,0:T(2,128)(2,1)}), bf16[16,2,8192]{2,1,0:T(2,128)(2,1)}, u32[]{:S(2)}, u32[]{:S(2)}) async-start(bf16[16,2,8192]{2,1,0:T(2,128)(2,1)} %reshape.348), calls=%async_computation | async-start | bytes 1048576 | tf_op jit(solution)/shard_map/all_to_all | solution.py:97
  258.9 4.3 %gather_fusion = bf16[2,2048,2,128]{3,1,2,0:T(8,128)(2,1)S(1)} fusion(bf16[8,2048,2,128]{3,1,2,0:T(8,128)(2,1)} %bitcast.51, s32[1024]{0:T(1024)S(1)} %pad_clamp_fusion), kind=kCustom, calls=%fused_computation | custom fusion | bytes 4194312 | tf_op jit(solution)/shard_map/jit(_take)/gather | solution.py:120
  263.4 2.2 bitcast_select_fusion
  265.6 6.7 %multiply_reduce_fusion.1 = (f32[4096]{0:T(1024)S(1)}, f32[4096,128]{1,0:T(8,128)S(1)}) fusion(bf16[4096,1536]{1,0:T(8,128)(2,1)} %bitcast.249, bf16[1536,128]{1,0:T(8,128)(2,1)S(1)} %copy-done), kind=kOutput, calls=%fused_computation.63 | convolution fusion | flops 1611657216 | bytes 15089664 | tf_op jit(solution)/shard_map/dot_general | solution.py:37
  272.3 1.6 copy-done.19
  273.9 3.5 multiply_reduce_fusion
  277.4 3.4 convolution_convert_fusion
  282.4 2.0 pad_maximum_fusion
  284.4 2.5 reshape.328
  286.9 51.6 %while.39 = (s32[]{:T(128)}, bf16[2,2048,128]{2,1,0:T(8,128)(2,1)}, bf16[2,2048,3,128]{3,1,2,0:T(8,128)(2,1)}, bf16[2,4096,2,128]{3,1,2,0:T(8,128)(2,1)}, s32[]{:T(128)}, /*index=5*/s32[]{:T(128)}, s32[]{:T(128)}) while((s32[]{:T(128)}, bf16[2,2048,128]{2,1,0:T(8,128)(2,1)}, bf16[2,2048,3,128]{3,1,2,0:T(8,128)(2,1)}, ...), condition=%wide.region_15.16_spmd, body=%wide.region_11.15_spmd.sunk | while | flops 1632697856 | bytes 73667344 | solution.py:136
  287.1 1.7 dynamic-slice_bitcast_fusion.4
  288.9 0.9 copy-done.2
  290.0 1.4 maximum_bitcast_fusion.4
  291.5 20.4 %while.40 = (s32[]{:T(128)}, bf16[4,512,1,128]{3,1,2,0:T(8,128)(2,1)S(1)}, bf16[4,512,1,128]{3,1,2,0:T(8,128)(2,1)S(1)}, bf16[6144,1,128]{2,0,1:T(8,128)(2,1)S(1)}, bf16[6144,1,128]{2,0,1:T(8,128)(2,1)}, /*index=5*/s32[]{:T(128)}) while((s32[]{:T(128)}, bf16[4,512,1,128]{3,1,2,0:T(8,128)(2,1)S(1)}, bf16[4,512,1,128]{3,1,2,0:T(8,128)(2,1)S(1)}, ...), condition=%wide.region_14.14_spmd, body=%wide.region_12.13_spmd.sunk | while | flops 1626406400 | bytes 34869352 | solution.py:65
  291.5 2.0 fusion.114
  293.5 3.1 fusion.115
  296.6 2.0 fusion.114
  298.6 3.1 fusion.115
  301.7 2.0 fusion.114
  303.7 3.1 fusion.115
  306.8 2.0 fusion.114
  308.9 3.1 fusion.115
  311.9 0.9 constant_dynamic-update-slice_fusion.2
  312.8 1.7 dynamic-slice_bitcast_fusion.4
  314.5 0.9 copy-done.2
  315.7 1.4 maximum_bitcast_fusion.4
  317.2 20.5 %while.40 = (s32[]{:T(128)}, bf16[4,512,1,128]{3,1,2,0:T(8,128)(2,1)S(1)}, bf16[4,512,1,128]{3,1,2,0:T(8,128)(2,1)S(1)}, bf16[6144,1,128]{2,0,1:T(8,128)(2,1)S(1)}, bf16[6144,1,128]{2,0,1:T(8,128)(2,1)}, /*index=5*/s32[]{:T(128)}) while((s32[]{:T(128)}, bf16[4,512,1,128]{3,1,2,0:T(8,128)(2,1)S(1)}, bf16[4,512,1,128]{3,1,2,0:T(8,128)(2,1)S(1)}, ...), condition=%wide.region_14.14_spmd, body=%wide.region_12.13_spmd.sunk | while | flops 1626406400 | bytes 34869352 | solution.py:65
  317.2 2.0 fusion.114
  319.2 3.1 fusion.115
  322.3 2.0 fusion.114
  324.3 3.1 fusion.115
  327.4 2.0 fusion.114
  329.4 3.1 fusion.115
  332.5 2.0 fusion.114
  334.6 3.1 fusion.115
  338.5 3.7 copy.60
  342.1 5.7 %all-to-all-start.2 = ((bf16[2,2048,128]{2,0,1:T(2,128)(2,1)}), bf16[2,2048,128]{2,0,1:T(2,128)(2,1)S(1)}, u32[]{:S(2)}, u32[]{:S(2)}) async-start(bf16[2,2048,128]{2,0,1:T(2,128)(2,1)} %copy.60), calls=%async_computation.2 | async-start | bytes 2097152 | tf_op jit(solution)/shard_map/all_to_all | solution.py:97
  348.4 2.3 reshape.349
  351.1 4.6 %fusion.52 = bf16[1,128,1536]{2,1,0:T(8,128)(2,1)} fusion(bf16[128,2048]{0,1:T(8,128)(2,1)S(1)} %bitcast.242, bf16[2048,1536]{1,0:T(8,128)(2,1)} %all-gather.6.cloned.1.call-done, bf16[1,128,1536]{2,1,0:T(8,128)(2,1)S(1)} %copy-done.7, f32[1536]{0:T(1024)S(1)} %convolution_reduce_fusion.2), kind=kOutput, calls=%fused_computation.55 | convolution fusion | flops 806092800 | bytes 7608320 | tf_op jit(solution)/shard_map/dot_general | solution.py:99
  355.6 8.1 %all-to-all-done.2 = bf16[2,2048,128]{2,0,1:T(2,128)(2,1)S(1)} async-done(((bf16[2,2048,128]{2,0,1:T(2,128)(2,1)}), bf16[2,2048,128]{2,0,1:T(2,128)(2,1)S(1)}, u32[]{:S(2)}, u32[]{:S(2)}) %all-to-all-start.2) | async-done | bytes 1048608 | tf_op jit(solution)/shard_map/all_to_all | solution.py:97
  364.9 5.5 %fusion.48 = bf16[1,2,128,1536]{3,2,1,0:T(8,128)(2,1)} fusion(bf16[2,128,2048]{2,1,0:T(8,128)(2,1)S(1)} %dot_general.69, bf16[2048,1536]{1,0:T(8,128)(2,1)} %all-gather.6.cloned.1.call-done, bf16[1,2,128,1536]{3,2,1,0:T(8,128)(2,1)S(1)} %copy-done.6, f32[2,1536]{1,0:T(2,128)S(1)} %fusion.77), kind=kOutput, calls=%fused_computation.53 | convolution fusion | flops 1612185600 | bytes 8925184 | tf_op jit(solution)/shard_map/dot_general | solution.py:99
  (115 shorter events, 11.7 us)
Async XLA Ops:
  7.2 59.3 %copy-start = (bf16[1536,128]{1,0:T(8,128)(2,1)S(1)}, bf16[1536,128]{1,0:T(8,128)(2,1)}, u32[]{:S(2)}) copy-start(bf16[1536,128]{1,0:T(8,128)(2,1)} %param.28) | copy-start | bytes 1179652
  7.2 8.0 %copy-start.5 = (bf16[1,2,128,1536]{3,2,1,0:T(8,128)(2,1)S(1)}, bf16[1,2,128,1536]{3,2,1,0:T(8,128)(2,1)}, u32[]{:S(2)}) copy-start(bf16[1,2,128,1536]{3,2,1,0:T(8,128)(2,1)} %param.22) | copy-start | bytes 2359300
  7.2 53.9 %all-gather.4.cloned.1.call-start = ((), (), s32[]{:S(2)}) async-start(), calls=%async_computation.3 | async-start | bytes 6684672 | tf_op jit(solution)/shard_map/all_gather | solution.py:88
  9.2 6.5 %copy-start.8 = (f32[64,1536]{1,0:T(8,128)S(1)}, f32[64,1536]{1,0:T(8,128)}, u32[]{:S(2)}) copy-start(f32[64,1536]{1,0:T(8,128)} %param.26) | copy-start | bytes 1179652
  9.2 6.5 %copy-start.13 = (s32[1,2]{1,0:T(1,128)S(1)}, s32[1,2]{1,0:T(1,128)}, u32[]{:S(2)}) copy-start(s32[1,2]{1,0:T(1,128)} %param.23) | copy-start | bytes 28
  9.3 6.7 %copy-start.9 = (f32[64,1536]{1,0:T(8,128)S(1)}, f32[64,1536]{1,0:T(8,128)}, u32[]{:S(2)}) copy-start(f32[64,1536]{1,0:T(8,128)} %param.25) | copy-start | bytes 1179652
  15.1 250.5 %all-gather.8.cloned.1.call-start = ((), (), s32[]{:S(2)}) async-start(), calls=%async_computation.5 | async-start | bytes 13369344 | tf_op jit(solution)/shard_map/all_gather | solution.py:88
  15.3 45.8 %copy-start.11 = (bf16[1536,128]{1,0:T(8,128)(2,1)S(1)}, bf16[1536,128]{1,0:T(8,128)(2,1)}, u32[]{:S(2)}) copy-start(bf16[1536,128]{1,0:T(8,128)(2,1)} %param.29) | copy-start | bytes 1179652
  66.4 4.9 %copy-start.4 = (bf16[1,2048,1536]{2,1,0:T(8,128)(2,1)S(1)}, bf16[1,2048,1536]{2,1,0:T(8,128)(2,1)}, u32[]{:S(2)}) copy-start(bf16[1,2048,1536]{2,1,0:T(8,128)(2,1)} %all-gather.4.cloned.1.call-done) | copy-start | bytes 18874372
  66.5 4.9 %copy-start.20 = (bf16[1536,128]{1,0:T(8,128)(2,1)S(1)}, bf16[1536,128]{1,0:T(8,128)(2,1)}, u32[]{:S(2)}) copy-start(bf16[1536,128]{1,0:T(8,128)(2,1)} %param.30) | copy-start | bytes 1179652
  71.3 1.8 copy-start.15
  71.3 2.2 copy-start.17
  79.0 7.4 %copy-start.22 = (s32[1,2]{1,0:T(1,128)S(1)}, s32[1,2]{1,0:T(1,128)}, u32[]{:S(2)}) copy-start(s32[1,2]{1,0:T(1,128)} %param.24) | copy-start | bytes 28
  79.0 174.1 %all-to-all-start.1 = ((bf16[8,1,2048,2,128]{4,2,3,1,0:T(8,128)(2,1)}), bf16[8,1,2048,2,128]{4,2,3,1,0:T(8,128)(2,1)}, u32[]{:S(2)}, u32[]{:S(2)}) async-start(bf16[8,1,2048,2,128]{4,2,3,1,0:T(8,128)(2,1)} %stack.14), calls=%async_computation.1 | async-start | bytes 16777216 | tf_op jit(solution)/shard_map/all_to_all | solution.py:115
  85.7 265.4 %all-gather.6.cloned.1.call-start = ((), (), s32[]{:S(2)}) async-start(), calls=%async_computation.4 | async-start | bytes 6684672 | tf_op jit(solution)/shard_map/all_gather | solution.py:84
  253.1 89.0 %all-to-all-start = ((bf16[16,2,8192]{2,1,0:T(2,128)(2,1)}), bf16[16,2,8192]{2,1,0:T(2,128)(2,1)}, u32[]{:S(2)}, u32[]{:S(2)}) async-start(bf16[16,2,8192]{2,1,0:T(2,128)(2,1)} %reshape.348), calls=%async_computation | async-start | bytes 1048576 | tf_op jit(solution)/shard_map/all_to_all | solution.py:97
  265.6 6.7 %copy-start.12 = (bf16[1536,128]{1,0:T(8,128)(2,1)S(1)}, bf16[1536,128]{1,0:T(8,128)(2,1)}, u32[]{:S(2)}) copy-start(bf16[1536,128]{1,0:T(8,128)(2,1)} %param.29) | copy-start | bytes 1179652
  265.6 8.3 %copy-start.19 = (bf16[2,2048,1536]{2,1,0:T(8,128)(2,1)S(1)}, bf16[2,2048,1536]{2,1,0:T(8,128)(2,1)}, u32[]{:S(2)}) copy-start(bf16[2,2048,1536]{2,1,0:T(8,128)(2,1)} %all-gather.8.cloned.1.call-done) | copy-start | bytes 37748740
  273.9 3.5 copy-start.21
  277.4 3.5 copy-start.16
  280.9 0.8 copy-start.18
  287.1 2.7 copy-start.2
  291.5 2.0 copy-start.3
  296.6 2.0 copy-start.3
  301.7 2.0 copy-start.3
  306.8 2.0 copy-start.3
  312.8 2.7 copy-start.2
  317.2 2.0 copy-start.3
  322.3 2.0 copy-start.3
  327.4 2.0 copy-start.3
  332.5 2.0 copy-start.3
  338.5 9.4 %copy-start.10 = (f32[64,1536]{1,0:T(8,128)S(1)}, f32[64,1536]{1,0:T(8,128)}, u32[]{:S(2)}) copy-start(f32[64,1536]{1,0:T(8,128)} %param.27) | copy-start | bytes 1179652
  338.5 9.7 %copy-start.14 = (s32[1,2]{1,0:T(1,128)S(1)}, s32[1,2]{1,0:T(1,128)}, u32[]{:S(2)}) copy-start(s32[1,2]{1,0:T(1,128)} %param.23) | copy-start | bytes 28
  342.1 21.6 %all-to-all-start.2 = ((bf16[2,2048,128]{2,0,1:T(2,128)(2,1)}), bf16[2,2048,128]{2,0,1:T(2,128)(2,1)S(1)}, u32[]{:S(2)}, u32[]{:S(2)}) async-start(bf16[2,2048,128]{2,0,1:T(2,128)(2,1)} %copy.60), calls=%async_computation.2 | async-start | bytes 2097152 | tf_op jit(solution)/shard_map/all_to_all | solution.py:97
  348.4 2.7 copy-start.7
  363.7 1.2 copy-start.6
  364.9 5.5 %copy-start.1 = (bf16[1536,128]{1,0:T(8,128)(2,1)S(1)}, bf16[1536,128]{1,0:T(8,128)(2,1)}, u32[]{:S(2)}) copy-start(bf16[1536,128]{1,0:T(8,128)(2,1)} %param.28) | copy-start | bytes 1179652
Sparse Core Ops, SparseCore 0:
  15.2 45.8 all-gather.3
  63.3 119.5 all-gather.7
  184.6 70.6 all-gather.5
